TPU v7x, 32 devices: a whole 2x2x4 slice. The times are simulated.
32 devices in a mesh: inner: 4 (over x, core), outer: 2 (over y), tile: 4 (over z).
Axes of the slice: x: 2, y: 2, z: 4, core: 2. Of those that a mesh axis runs over, the one named last changes fastest.
Arguments:
- density: bfloat16 [128, 256, 2048], P(('inner', 'outer'), None, 'tile'), parts along dimension 2, may hold values from 0.049804688 to 1
- extinction: float32 [128], P(('inner', 'outer')), may hold values from 0.0002 to 0.01
- occupancy: int32 [8, 16, 128], P(('inner', 'outer'), None, 'tile'), parts along dimension 2, may hold values 0 or 1
- colour_slope: float32 [3], replicated, may hold values from -6 to 6
- slab_rank: int32 [8], replicated, may hold values from 0 to 7, as said below
Outputs:
- image: float32 [4, 256, 2048], P(None, 'inner', ('tile', 'outer')), parts along dimension 2
There are 4 independent parts, one for each index of `tile`. A program takes and returns all parts, laid end to end along the dimension named above; an argument that names none is the same for every part. Nothing has to cross between parts.
Inputs may be any that keep to these rules, and one draw needn't show every extreme that they name: slab_rank is a permutation of 0 to 7; the slabs whose index leaves the same remainder modulo 2 hold 4 consecutive ranks.
All inputs are finite; a program needn't handle non-finite values. No bound on the sum of `occupancy` on one device may be relied on, other than what follows from the above.
Results may differ from a plain program's by a relative error of at most 0.0003.
Values sent between devices are 32-bit elements; how exact they have to be, the bound alone decides.
A program may use at most 64 MiB of HBM per device.

v0:
```python
import jax
import jax.numpy as jnp
from jax import lax
from jax.sharding import PartitionSpec as P


def march(density, extinction, occupancy, colour_slope):
    blocks = occupancy[0].astype(jnp.float32)
    filled = jnp.repeat(
        jnp.repeat(blocks, density.shape[1] // blocks.shape[0], axis=0),
        density.shape[2] // blocks.shape[1],
        axis=1,
    )

    def advance(carry, inputs):
        colour_sum, through = carry
        layer, absorb = inputs
        sample = layer.astype(jnp.float32) * filled
        opacity = 1.0 - jnp.exp(-absorb * sample)
        colour = jax.nn.sigmoid(colour_slope[:, None, None] * (sample - 0.3))
        colour_sum = colour_sum + (through * opacity)[None] * colour
        through = through * (1.0 - opacity)
        return ((colour_sum, through), None)

    start = (
        jnp.zeros((3,) + density.shape[1:], jnp.float32),
        jnp.ones(density.shape[1:], jnp.float32),
    )
    (colour_sum, through), unused = lax.scan(advance, start, (density, extinction))
    return jnp.concatenate([colour_sum, through[None]], axis=0)


def composite(pieces, ranks):
    count = pieces.shape[0]
    select = (ranks[None, :] == jnp.arange(count, dtype=jnp.int32)[:, None]).astype(jnp.float32)
    ordered = jnp.einsum("kj,jchw->kchw", select, pieces, precision=lax.Precision.HIGHEST)
    running = jnp.cumprod(ordered[:, 3], axis=0)
    front = jnp.concatenate([jnp.ones_like(running[:1]), running[:-1]], axis=0)
    colour = jnp.sum(ordered[:, :3] * front[:, None], axis=0)
    return jnp.concatenate([colour, running[-1:]], axis=0)


def shards(density, extinction, occupancy, colour_slope, slab_rank):
    pieces = march(density, extinction, occupancy, colour_slope)
    inner_count = lax.axis_size("inner")
    outer_count = lax.axis_size("outer")
    rank_grid = slab_rank.reshape(inner_count, outer_count)
    mine = lax.dynamic_index_in_dim(rank_grid, lax.axis_index("outer"), 1, keepdims=False)
    arrived = lax.all_to_all(pieces[None], "inner", split_axis=2, concat_axis=0, tiled=True)
    banded = composite(arrived, mine - jnp.min(mine))
    group_rank = jnp.min(rank_grid, axis=0) // inner_count
    arrived_groups = lax.all_to_all(banded[None], "outer", split_axis=3, concat_axis=0, tiled=True)
    total = composite(arrived_groups, group_rank)
    return jnp.concatenate([total[:3], 1.0 - total[3:]], axis=0)


def solution(mesh):
    placed = (
        P(("inner", "outer"), None, "tile"),
        P(("inner", "outer")),
        P(("inner", "outer"), None, "tile"),
        P(),
        P(),
    )
    return jax.shard_map(
        shards,
        mesh=mesh,
        in_specs=placed,
        out_specs=P(None, "inner", ("tile", "outer")),
        check_vma=False,
    )
```

profile of v0, /device:TPU:0, one launch (start us, length us, event | category | flops | bytes accessed | tf_op | source)
XLA Modules:
  0.0 172.9 jit_solution(8837379326745376586)
XLA Ops:
  0.8 95.0 %while.15 = (s32[]{:T(128)}, f32[3,256,512]{2,1,0:T(8,128)S(1)}, f32[256,512]{0,1:T(8,128)}, f32[16]{0:T(128)}, bf16[16,256,512]{2,1,0:T(8,128)(2,1)}, /*index=5...) while((s32[]{:T(128)}, f32[3,256,512]{2,1,0:T(8,128)S(1)}, f32[256,512]{0,1:T(8,128)}, ...), condition=%wide.region_3.4_spmd.clone, body=%wide.region_2.3_spmd.clone.sunk | while | flops 4194308 | bytes 10027520 | solution.py:29
  0.8 1.0 constant_dynamic-slice_fusion.2
  3.6 1.0 fusion.30
  4.8 1.0 select_add_fusion.2
  5.8 1.0 constant_dynamic-slice_fusion.2
  8.5 2.0 %fusion.30 = (f32[256,512]{0,1:T(8,128)}, f32[256,512]{0,1:T(8,128)S(1)}) fusion(bf16[1,256,512]{1,2,0:T(8,128)(2,1)S(1)} %copy.83, f32[256,512]{0,1:T(8,128)} %get-tuple-element.235, f32[256,32]{0,1:T(8,128)S(1)} %get-tuple-element.248, f32[]{:T(128)} %bitcast.77, pred[]{:T(512)S(6)} %compare.12), kind=kLoop, calls=%fused_computation.12.clone.1 | loop fusion | flops 1048576 | bytes 1867781 | tf_op jit(solution)/shard_map/while/body/eval_jaxpr/mul | solution.py:22
  11.8 1.0 constant_dynamic-slice_fusion.2
  14.5 2.0 %fusion.30 = (f32[256,512]{0,1:T(8,128)}, f32[256,512]{0,1:T(8,128)S(1)}) fusion(bf16[1,256,512]{1,2,0:T(8,128)(2,1)S(1)} %copy.83, f32[256,512]{0,1:T(8,128)} %get-tuple-element.235, f32[256,32]{0,1:T(8,128)S(1)} %get-tuple-element.248, f32[]{:T(128)} %bitcast.77, pred[]{:T(512)S(6)} %compare.12), kind=kLoop, calls=%fused_computation.12.clone.1 | loop fusion | flops 1048576 | bytes 1867781 | tf_op jit(solution)/shard_map/while/body/eval_jaxpr/mul | solution.py:22
  17.8 1.0 constant_dynamic-slice_fusion.2
  20.5 2.0 %fusion.30 = (f32[256,512]{0,1:T(8,128)}, f32[256,512]{0,1:T(8,128)S(1)}) fusion(bf16[1,256,512]{1,2,0:T(8,128)(2,1)S(1)} %copy.83, f32[256,512]{0,1:T(8,128)} %get-tuple-element.235, f32[256,32]{0,1:T(8,128)S(1)} %get-tuple-element.248, f32[]{:T(128)} %bitcast.77, pred[]{:T(512)S(6)} %compare.12), kind=kLoop, calls=%fused_computation.12.clone.1 | loop fusion | flops 1048576 | bytes 1867781 | tf_op jit(solution)/shard_map/while/body/eval_jaxpr/mul | solution.py:22
  23.8 1.0 constant_dynamic-slice_fusion.2
  26.5 2.0 %fusion.30 = (f32[256,512]{0,1:T(8,128)}, f32[256,512]{0,1:T(8,128)S(1)}) fusion(bf16[1,256,512]{1,2,0:T(8,128)(2,1)S(1)} %copy.83, f32[256,512]{0,1:T(8,128)} %get-tuple-element.235, f32[256,32]{0,1:T(8,128)S(1)} %get-tuple-element.248, f32[]{:T(128)} %bitcast.77, pred[]{:T(512)S(6)} %compare.12), kind=kLoop, calls=%fused_computation.12.clone.1 | loop fusion | flops 1048576 | bytes 1867781 | tf_op jit(solution)/shard_map/while/body/eval_jaxpr/mul | solution.py:22
  29.8 1.0 constant_dynamic-slice_fusion.2
  32.5 2.0 %fusion.30 = (f32[256,512]{0,1:T(8,128)}, f32[256,512]{0,1:T(8,128)S(1)}) fusion(bf16[1,256,512]{1,2,0:T(8,128)(2,1)S(1)} %copy.83, f32[256,512]{0,1:T(8,128)} %get-tuple-element.235, f32[256,32]{0,1:T(8,128)S(1)} %get-tuple-element.248, f32[]{:T(128)} %bitcast.77, pred[]{:T(512)S(6)} %compare.12), kind=kLoop, calls=%fused_computation.12.clone.1 | loop fusion | flops 1048576 | bytes 1867781 | tf_op jit(solution)/shard_map/while/body/eval_jaxpr/mul | solution.py:22
  35.8 1.0 constant_dynamic-slice_fusion.2
  38.5 2.0 %fusion.30 = (f32[256,512]{0,1:T(8,128)}, f32[256,512]{0,1:T(8,128)S(1)}) fusion(bf16[1,256,512]{1,2,0:T(8,128)(2,1)S(1)} %copy.83, f32[256,512]{0,1:T(8,128)} %get-tuple-element.235, f32[256,32]{0,1:T(8,128)S(1)} %get-tuple-element.248, f32[]{:T(128)} %bitcast.77, pred[]{:T(512)S(6)} %compare.12), kind=kLoop, calls=%fused_computation.12.clone.1 | loop fusion | flops 1048576 | bytes 1867781 | tf_op jit(solution)/shard_map/while/body/eval_jaxpr/mul | solution.py:22
  41.8 1.0 constant_dynamic-slice_fusion.2
  44.5 2.0 %fusion.30 = (f32[256,512]{0,1:T(8,128)}, f32[256,512]{0,1:T(8,128)S(1)}) fusion(bf16[1,256,512]{1,2,0:T(8,128)(2,1)S(1)} %copy.83, f32[256,512]{0,1:T(8,128)} %get-tuple-element.235, f32[256,32]{0,1:T(8,128)S(1)} %get-tuple-element.248, f32[]{:T(128)} %bitcast.77, pred[]{:T(512)S(6)} %compare.12), kind=kLoop, calls=%fused_computation.12.clone.1 | loop fusion | flops 1048576 | bytes 1867781 | tf_op jit(solution)/shard_map/while/body/eval_jaxpr/mul | solution.py:22
  47.8 1.0 constant_dynamic-slice_fusion.2
  50.5 2.0 %fusion.30 = (f32[256,512]{0,1:T(8,128)}, f32[256,512]{0,1:T(8,128)S(1)}) fusion(bf16[1,256,512]{1,2,0:T(8,128)(2,1)S(1)} %copy.83, f32[256,512]{0,1:T(8,128)} %get-tuple-element.235, f32[256,32]{0,1:T(8,128)S(1)} %get-tuple-element.248, f32[]{:T(128)} %bitcast.77, pred[]{:T(512)S(6)} %compare.12), kind=kLoop, calls=%fused_computation.12.clone.1 | loop fusion | flops 1048576 | bytes 1867781 | tf_op jit(solution)/shard_map/while/body/eval_jaxpr/mul | solution.py:22
  53.8 1.0 constant_dynamic-slice_fusion.2
  56.5 2.0 %fusion.30 = (f32[256,512]{0,1:T(8,128)}, f32[256,512]{0,1:T(8,128)S(1)}) fusion(bf16[1,256,512]{1,2,0:T(8,128)(2,1)S(1)} %copy.83, f32[256,512]{0,1:T(8,128)} %get-tuple-element.235, f32[256,32]{0,1:T(8,128)S(1)} %get-tuple-element.248, f32[]{:T(128)} %bitcast.77, pred[]{:T(512)S(6)} %compare.12), kind=kLoop, calls=%fused_computation.12.clone.1 | loop fusion | flops 1048576 | bytes 1867781 | tf_op jit(solution)/shard_map/while/body/eval_jaxpr/mul | solution.py:22
  59.8 1.0 constant_dynamic-slice_fusion.2
  62.5 2.0 %fusion.30 = (f32[256,512]{0,1:T(8,128)}, f32[256,512]{0,1:T(8,128)S(1)}) fusion(bf16[1,256,512]{1,2,0:T(8,128)(2,1)S(1)} %copy.83, f32[256,512]{0,1:T(8,128)} %get-tuple-element.235, f32[256,32]{0,1:T(8,128)S(1)} %get-tuple-element.248, f32[]{:T(128)} %bitcast.77, pred[]{:T(512)S(6)} %compare.12), kind=kLoop, calls=%fused_computation.12.clone.1 | loop fusion | flops 1048576 | bytes 1867781 | tf_op jit(solution)/shard_map/while/body/eval_jaxpr/mul | solution.py:22
  65.8 1.0 constant_dynamic-slice_fusion.2
  68.5 2.0 %fusion.30 = (f32[256,512]{0,1:T(8,128)}, f32[256,512]{0,1:T(8,128)S(1)}) fusion(bf16[1,256,512]{1,2,0:T(8,128)(2,1)S(1)} %copy.83, f32[256,512]{0,1:T(8,128)} %get-tuple-element.235, f32[256,32]{0,1:T(8,128)S(1)} %get-tuple-element.248, f32[]{:T(128)} %bitcast.77, pred[]{:T(512)S(6)} %compare.12), kind=kLoop, calls=%fused_computation.12.clone.1 | loop fusion | flops 1048576 | bytes 1867781 | tf_op jit(solution)/shard_map/while/body/eval_jaxpr/mul | solution.py:22
  71.8 1.0 constant_dynamic-slice_fusion.2
  74.5 2.0 %fusion.30 = (f32[256,512]{0,1:T(8,128)}, f32[256,512]{0,1:T(8,128)S(1)}) fusion(bf16[1,256,512]{1,2,0:T(8,128)(2,1)S(1)} %copy.83, f32[256,512]{0,1:T(8,128)} %get-tuple-element.235, f32[256,32]{0,1:T(8,128)S(1)} %get-tuple-element.248, f32[]{:T(128)} %bitcast.77, pred[]{:T(512)S(6)} %compare.12), kind=kLoop, calls=%fused_computation.12.clone.1 | loop fusion | flops 1048576 | bytes 1867781 | tf_op jit(solution)/shard_map/while/body/eval_jaxpr/mul | solution.py:22
  77.8 1.0 constant_dynamic-slice_fusion.2
  80.5 2.0 %fusion.30 = (f32[256,512]{0,1:T(8,128)}, f32[256,512]{0,1:T(8,128)S(1)}) fusion(bf16[1,256,512]{1,2,0:T(8,128)(2,1)S(1)} %copy.83, f32[256,512]{0,1:T(8,128)} %get-tuple-element.235, f32[256,32]{0,1:T(8,128)S(1)} %get-tuple-element.248, f32[]{:T(128)} %bitcast.77, pred[]{:T(512)S(6)} %compare.12), kind=kLoop, calls=%fused_computation.12.clone.1 | loop fusion | flops 1048576 | bytes 1867781 | tf_op jit(solution)/shard_map/while/body/eval_jaxpr/mul | solution.py:22
  83.8 1.0 constant_dynamic-slice_fusion.2
  86.5 2.0 %fusion.30 = (f32[256,512]{0,1:T(8,128)}, f32[256,512]{0,1:T(8,128)S(1)}) fusion(bf16[1,256,512]{1,2,0:T(8,128)(2,1)S(1)} %copy.83, f32[256,512]{0,1:T(8,128)} %get-tuple-element.235, f32[256,32]{0,1:T(8,128)S(1)} %get-tuple-element.248, f32[]{:T(128)} %bitcast.77, pred[]{:T(512)S(6)} %compare.12), kind=kLoop, calls=%fused_computation.12.clone.1 | loop fusion | flops 1048576 | bytes 1867781 | tf_op jit(solution)/shard_map/while/body/eval_jaxpr/mul | solution.py:22
  89.8 1.0 constant_dynamic-slice_fusion.2
  92.5 2.0 %fusion.30 = (f32[256,512]{0,1:T(8,128)}, f32[256,512]{0,1:T(8,128)S(1)}) fusion(bf16[1,256,512]{1,2,0:T(8,128)(2,1)S(1)} %copy.83, f32[256,512]{0,1:T(8,128)} %get-tuple-element.235, f32[256,32]{0,1:T(8,128)S(1)} %get-tuple-element.248, f32[]{:T(128)} %bitcast.77, pred[]{:T(512)S(6)} %compare.12), kind=kLoop, calls=%fused_computation.12.clone.1 | loop fusion | flops 1048576 | bytes 1867781 | tf_op jit(solution)/shard_map/while/body/eval_jaxpr/mul | solution.py:22
  95.7 1.3 copy.67
  97.0 1.1 copy.57
  98.1 2.3 %maximum_bitcast_fusion = f32[1,4,256,512]{3,1,0,2:T(4,128)} fusion(f32[1,256,512]{2,0,1:T(1,128)S(1)} %copy.67, f32[3,256,512]{2,0,1:T(4,128)S(1)} %copy.57), kind=kLoop, calls=%fused_computation.14 | loop fusion | flops 524288 | bytes 4194304 | tf_op jit(solution)/shard_map/broadcast_in_dim | solution.py:49
  100.4 4.3 %all-to-all-start = ((f32[1,4,256,512]{3,1,0,2:T(4,128)}), f32[1,4,256,512]{3,1,0,2:T(4,128)S(1)}, u32[]{:S(2)}, u32[]{:S(2)}) async-start(f32[1,4,256,512]{3,1,0,2:T(4,128)} %maximum_bitcast_fusion), calls=%async_computation | async-start | bytes 4194304 | tf_op jit(solution)/shard_map/all_to_all | solution.py:49
  106.4 24.2 %all-to-all-done = f32[1,4,256,512]{3,1,0,2:T(4,128)S(1)} async-done(((f32[1,4,256,512]{3,1,0,2:T(4,128)}), f32[1,4,256,512]{3,1,0,2:T(4,128)S(1)}, u32[]{:S(2)}, u32[]{:S(2)}) %all-to-all-start) | async-done | bytes 2097184 | tf_op jit(solution)/shard_map/all_to_all | solution.py:49
  130.6 3.2 %fusion.11 = f32[4,4,64,512]{3,0,2,1:T(4,128)S(1)} fusion(f32[1,4,4,64,512]{4,1,3,2,0:T(4,128)S(1)} %bitcast.78, s32[4]{0:T(128)S(1)} %subtract_reduce_fusion), kind=kOutput, calls=%fused_computation.15 | convolution fusion | flops 25165840 | bytes 4194320 | tf_op jit(solution)/shard_map/kj,jchw->kchw/dot_general | solution.py:36
  133.9 1.3 copy-done
  135.3 14.9 %reduce_window.18 = f32[4,64,512]{2,0,1:T(4,128)S(1)} reduce-window(f32[4,64,512]{2,0,1:T(4,128)S(1)} %slice_bitcast_fusion, f32[]{:T(128)} %constant.68.clone.1), window={size=4x1x1 pad=3_0x0_0x0_0}, to_apply=%region_4.5 | reduce-window | flops 393216 | bytes 1048580 | tf_op jit(solution)/shard_map/jit(cumprod)/reduce_window | solution.py:37
  150.5 1.2 fusion.14
  152.2 1.7 reshape.60
  153.9 3.7 %all-to-all-start.1 = ((f32[2,1,65536]{2,1,0:T(1,128)}), f32[2,1,65536]{2,1,0:T(1,128)S(1)}, u32[]{:S(2)}, u32[]{:S(2)}) async-start(f32[2,1,65536]{2,1,0:T(1,128)} %reshape.60), calls=%async_computation.1 | async-start | bytes 1048576 | tf_op jit(solution)/shard_map/all_to_all | solution.py:52
  157.7 8.4 %all-to-all-done.1 = f32[2,1,65536]{2,1,0:T(1,128)S(1)} async-done(((f32[2,1,65536]{2,1,0:T(1,128)}), f32[2,1,65536]{2,1,0:T(1,128)S(1)}, u32[]{:S(2)}, u32[]{:S(2)}) %all-to-all-start.1) | async-done | bytes 524320 | tf_op jit(solution)/shard_map/all_to_all | solution.py:52
  166.6 2.3 %reduce.3 = f32[2,65536]{1,0:T(2,128)S(1)} reduce(f32[2,1,65536]{2,1,0:T(1,128)S(1)} %all-to-all-done.1, f32[]{:T(128)} %broadcast.101), dimensions={1}, to_apply=%all_to_all.30.reduce_sub_computation | reduce | bytes 1048580 | tf_op jit(solution)/shard_map/all_to_all | solution.py:52
  170.4 1.1 fusion.15
  (190 shorter events, 41.2 us)
Async XLA Ops:
  0.8 1.4 copy-start.4
  2.2 2.6 %copy-start.2 = (f32[3]{0:T(128)S(1)}, f32[3]{0:T(128)}, u32[]{:S(2)}) copy-start(f32[3]{0:T(128)} %get-tuple-element.247) | copy-start | bytes 40 | tf_op jit(solution)/shard_map/while
  5.8 1.4 copy-start.4
  7.2 3.6 %copy-start.2 = (f32[3]{0:T(128)S(1)}, f32[3]{0:T(128)}, u32[]{:S(2)}) copy-start(f32[3]{0:T(128)} %get-tuple-element.247) | copy-start | bytes 40 | tf_op jit(solution)/shard_map/while
  11.8 1.4 copy-start.4
  13.2 3.6 %copy-start.2 = (f32[3]{0:T(128)S(1)}, f32[3]{0:T(128)}, u32[]{:S(2)}) copy-start(f32[3]{0:T(128)} %get-tuple-element.247) | copy-start | bytes 40 | tf_op jit(solution)/shard_map/while
  17.8 1.4 copy-start.4
  19.2 3.6 %copy-start.2 = (f32[3]{0:T(128)S(1)}, f32[3]{0:T(128)}, u32[]{:S(2)}) copy-start(f32[3]{0:T(128)} %get-tuple-element.247) | copy-start | bytes 40 | tf_op jit(solution)/shard_map/while
  23.7 1.4 copy-start.4
  25.2 3.6 %copy-start.2 = (f32[3]{0:T(128)S(1)}, f32[3]{0:T(128)}, u32[]{:S(2)}) copy-start(f32[3]{0:T(128)} %get-tuple-element.247) | copy-start | bytes 40 | tf_op jit(solution)/shard_map/while
  29.7 1.4 copy-start.4
  31.2 3.6 %copy-start.2 = (f32[3]{0:T(128)S(1)}, f32[3]{0:T(128)}, u32[]{:S(2)}) copy-start(f32[3]{0:T(128)} %get-tuple-element.247) | copy-start | bytes 40 | tf_op jit(solution)/shard_map/while
  35.7 1.4 copy-start.4
  37.2 3.6 %copy-start.2 = (f32[3]{0:T(128)S(1)}, f32[3]{0:T(128)}, u32[]{:S(2)}) copy-start(f32[3]{0:T(128)} %get-tuple-element.247) | copy-start | bytes 40 | tf_op jit(solution)/shard_map/while
  41.7 1.4 copy-start.4
  43.2 3.6 %copy-start.2 = (f32[3]{0:T(128)S(1)}, f32[3]{0:T(128)}, u32[]{:S(2)}) copy-start(f32[3]{0:T(128)} %get-tuple-element.247) | copy-start | bytes 40 | tf_op jit(solution)/shard_map/while
  47.7 1.4 copy-start.4
  49.2 3.6 %copy-start.2 = (f32[3]{0:T(128)S(1)}, f32[3]{0:T(128)}, u32[]{:S(2)}) copy-start(f32[3]{0:T(128)} %get-tuple-element.247) | copy-start | bytes 40 | tf_op jit(solution)/shard_map/while
  53.7 1.4 copy-start.4
  55.1 3.6 %copy-start.2 = (f32[3]{0:T(128)S(1)}, f32[3]{0:T(128)}, u32[]{:S(2)}) copy-start(f32[3]{0:T(128)} %get-tuple-element.247) | copy-start | bytes 40 | tf_op jit(solution)/shard_map/while
  59.7 1.4 copy-start.4
  61.1 3.6 %copy-start.2 = (f32[3]{0:T(128)S(1)}, f32[3]{0:T(128)}, u32[]{:S(2)}) copy-start(f32[3]{0:T(128)} %get-tuple-element.247) | copy-start | bytes 40 | tf_op jit(solution)/shard_map/while
  65.7 1.4 copy-start.4
  67.1 3.6 %copy-start.2 = (f32[3]{0:T(128)S(1)}, f32[3]{0:T(128)}, u32[]{:S(2)}) copy-start(f32[3]{0:T(128)} %get-tuple-element.247) | copy-start | bytes 40 | tf_op jit(solution)/shard_map/while
  71.7 1.4 copy-start.4
  73.1 3.6 %copy-start.2 = (f32[3]{0:T(128)S(1)}, f32[3]{0:T(128)}, u32[]{:S(2)}) copy-start(f32[3]{0:T(128)} %get-tuple-element.247) | copy-start | bytes 40 | tf_op jit(solution)/shard_map/while
  77.7 1.4 copy-start.4
  79.1 3.6 %copy-start.2 = (f32[3]{0:T(128)S(1)}, f32[3]{0:T(128)}, u32[]{:S(2)}) copy-start(f32[3]{0:T(128)} %get-tuple-element.247) | copy-start | bytes 40 | tf_op jit(solution)/shard_map/while
  83.7 1.4 copy-start.4
  85.1 3.6 %copy-start.2 = (f32[3]{0:T(128)S(1)}, f32[3]{0:T(128)}, u32[]{:S(2)}) copy-start(f32[3]{0:T(128)} %get-tuple-element.247) | copy-start | bytes 40 | tf_op jit(solution)/shard_map/while
  89.7 1.4 copy-start.4
  91.1 3.6 %copy-start.2 = (f32[3]{0:T(128)S(1)}, f32[3]{0:T(128)}, u32[]{:S(2)}) copy-start(f32[3]{0:T(128)} %get-tuple-element.247) | copy-start | bytes 40 | tf_op jit(solution)/shard_map/while
  100.4 4.3 %copy-start.3 = (s32[8]{0:T(128)S(1)}, s32[8]{0:T(128)}, u32[]{:S(2)}) copy-start(s32[8]{0:T(128)} %param.11) | copy-start | bytes 100
  100.4 30.2 %all-to-all-start = ((f32[1,4,256,512]{3,1,0,2:T(4,128)}), f32[1,4,256,512]{3,1,0,2:T(4,128)S(1)}, u32[]{:S(2)}, u32[]{:S(2)}) async-start(f32[1,4,256,512]{3,1,0,2:T(4,128)} %maximum_bitcast_fusion), calls=%async_computation | async-start | bytes 4194304 | tf_op jit(solution)/shard_map/all_to_all | solution.py:49
  133.9 1.4 copy-start
  135.3 15.2 %copy-start.1 = (f32[4,4,64,512]{3,0,2,1:T(4,128)S(1)}, f32[4,4,64,512]{3,0,2,1:T(4,128)}, u32[]{:S(2)}) copy-start(f32[4,4,64,512]{3,0,2,1:T(4,128)} %copy-done) | copy-start | bytes 6291460
  153.9 12.2 %all-to-all-start.1 = ((f32[2,1,65536]{2,1,0:T(1,128)}), f32[2,1,65536]{2,1,0:T(1,128)S(1)}, u32[]{:S(2)}, u32[]{:S(2)}) async-start(f32[2,1,65536]{2,1,0:T(1,128)} %reshape.60), calls=%async_computation.1 | async-start | bytes 1048576 | tf_op jit(solution)/shard_map/all_to_all | solution.py:52
where the time goes:
time: 174 us; the launch traced here: 173 us
  other arithmetic  71.8 us (41%)
  local copies, waits for them, and re-layouts  43.3 us (25%)
  waiting for transfers between devices  32.7 us (19%)
  loops' own time  12.6 us (7%)
  starting transfers between devices  8.05 us (5%)
  matrix products  4.3 us (2%)
    mul x16, other arithmetic, advance(): through = through * (1.0 - opacity)  31.2 us
    dynamic_slice x48, local copies, waits for them, and re-layouts, march(): lax.scan(advance, start, (density, extinction))  28.5 us
    all_to_all x1, waiting for transfers between devices, shards(): lax.all_to_all(pieces[None], 'inner', split_axis=2, concat_axis=0, tiled=...  24.2 us
    add x16, other arithmetic, advance(): colour_sum = colour_sum + (through * opacity)[None] * colour  15.3 us
    another operation x2, other arithmetic, composite(): running = jnp.cumprod(ordered[:, 3], axis=0)  15 us
    another operation x1, loops' own time, march(): lax.scan(advance, start, (density, extinction))  12.6 us
    all_to_all x1, waiting for transfers between devices, shards(): lax.all_to_all(banded[None], 'outer', split_axis=3, concat_axis=0, tiled=...  8.45 us
    all_to_all x1, starting transfers between devices, shards(): lax.all_to_all(pieces[None], 'inner', split_axis=2, concat_axis=0, tiled=...  4.34 us
  transfers between devices with their start and end apart: 2, of which 2 were waited for; matrix products, arithmetic and copies ran while one was open for 1% of the time, Pallas kernels for 0%

commit v1 on v0

--- a/solution.py
+++ b/solution.py
@@ -1,6 +1,10 @@
+import functools
+
 import jax
 import jax.numpy as jnp
 from jax import lax
+from jax.experimental import pallas as pl
+from jax.experimental.pallas import tpu as pltpu
 from jax.sharding import PartitionSpec as P
 
 
@@ -54,6 +58,239 @@
     return jnp.concatenate([total[:3], 1.0 - total[3:]], axis=0)
 
 
+ROWS = 16
+COLS = 256
+MESH = pl.DeviceIdType.MESH
+
+
+def fused_kernel(
+    inner_count, outer_count,
+    density, extinction, occupancy, slope, rank, out,
+    field, fill, pieces, arrived, banded, groups,
+    load_sem, send_sem, recv_sem, outer_send_sem, outer_recv_sem,
+):
+    slices, height, width = field.shape
+    band = height // inner_count
+    chunks = band // ROWS
+    part = width // outer_count
+    me = lax.axis_index("inner")
+    group = lax.axis_index("outer")
+
+    pairs = inner_count // 2
+    chip, core = me // 2, me % 2
+    partners = []
+    for step in range(1, pairs):
+        other = lax.rem(chip + step, pairs)
+        partners += [other * 2 + core, other * 2 + (1 - core)]
+    partners.append(chip * 2 + (1 - core))
+    outer_partners = [lax.rem(group + step, outer_count) for step in range(1, outer_count)]
+
+    def load(owner):
+        rows = pl.ds(pl.multiple_of(owner * band, ROWS), band)
+        return pltpu.make_async_copy(
+            density.at[:, rows, :], field.at[:, rows, :], load_sem.at[owner]
+        )
+
+    for owner in partners + [me]:
+        load(owner).start()
+
+    barrier = pltpu.get_barrier_semaphore()
+    for partner in partners:
+        pl.semaphore_signal(barrier, inc=1, device_id={"inner": partner}, device_id_type=MESH)
+    for partner in outer_partners:
+        pl.semaphore_signal(barrier, inc=1, device_id={"outer": partner}, device_id_type=MESH)
+
+    block_rows, block_columns = occupancy.shape[1:]
+    spread = (
+        lax.broadcasted_iota(jnp.int32, (block_columns, width), 1) // (width // block_columns)
+        == lax.broadcasted_iota(jnp.int32, (block_columns, width), 0)
+    ).astype(jnp.float32)
+    fill[...] = jnp.dot(
+        occupancy[0].astype(jnp.float32), spread, preferred_element_type=jnp.float32
+    )
+
+    half = [slope[k] * 0.5 for k in range(3)]
+    block_height = height // block_rows
+
+    def march(owner, chunk):
+        start = pl.multiple_of(owner * band + chunk * ROWS, ROWS)
+        to = pl.ds(pl.multiple_of(chunk * ROWS, ROWS), ROWS)
+        for column in range(0, width, COLS):
+            columns = slice(column, column + COLS)
+            through = jnp.ones((ROWS, COLS), jnp.float32)
+            sums = [jnp.zeros((ROWS, COLS), jnp.float32) for k in range(3)]
+            for t in range(slices):
+                sample = field[t, pl.ds(start, ROWS), columns].astype(jnp.float32)
+                after = through * jnp.exp2(sample * (extinction[t] * -1.4426950408889634))
+                weight = through - after
+                through = after
+                shifted = sample - 0.3
+                sums = [sums[k] + weight * jnp.tanh(half[k] * shifted) for k in range(3)]
+            full = fill[pl.ds(start // block_height, 1), columns] > 0.5
+            for k in range(3):
+                pieces[owner, k, to, columns] = jnp.where(
+                    full, 0.5 * ((1.0 - through) + sums[k]), 0.0
+                )
+            pieces[owner, 3, to, columns] = jnp.where(full, through, 1.0)
+
+    def rows_of(chunk):
+        return pl.ds(pl.multiple_of(chunk * ROWS, ROWS), ROWS)
+
+    def send(partner, chunk):
+        return pltpu.make_async_remote_copy(
+            src_ref=pieces.at[partner, :, rows_of(chunk), :],
+            dst_ref=arrived.at[me, :, rows_of(chunk), :],
+            send_sem=send_sem.at[partner, chunk],
+            recv_sem=recv_sem.at[me, chunk],
+            device_id={"inner": partner},
+            device_id_type=MESH,
+        )
+
+    def receive(partner, chunk):
+        return pltpu.make_async_remote_copy(
+            src_ref=pieces.at[partner, :, rows_of(chunk), :],
+            dst_ref=arrived.at[partner, :, rows_of(chunk), :],
+            send_sem=send_sem.at[partner, chunk],
+            recv_sem=recv_sem.at[partner, chunk],
+            device_id={"inner": partner},
+            device_id_type=MESH,
+        )
+
+    def outer_copy(partner, slot, chunk):
+        return pltpu.make_async_remote_copy(
+            src_ref=banded.at[:, rows_of(chunk), pl.ds(pl.multiple_of(partner * part, 128), part)],
+            dst_ref=groups.at[slot, :, rows_of(chunk), :],
+            send_sem=outer_send_sem.at[partner, chunk],
+            recv_sem=outer_recv_sem.at[slot, chunk],
+            device_id={"outer": partner},
+            device_id_type=MESH,
+        )
+
+    far = partners[:-1]
+    near = partners[-1]
+    for index, owner in enumerate(far):
+        load(owner).wait()
+        if index == 0:
+            pl.semaphore_wait(barrier, len(partners) + len(outer_partners))
+
+    @pl.loop(0, chunks)
+    def _(chunk):
+        for owner in far:
+            march(owner, chunk)
+            send(owner, chunk).start()
+
+    load(near).wait()
+    load(me).wait()
+
+    @pl.loop(0, chunks)
+    def _(chunk):
+        march(near, chunk)
+        send(near, chunk).start()
+        march(me, chunk)
+
+    def fronts(values, ranks):
+        found = []
+        for k in range(len(values)):
+            front = None
+            for j in range(len(values)):
+                if j != k:
+                    factor = jnp.where(ranks[j] < ranks[k], values[j], 1.0)
+                    front = factor if front is None else front * factor
+            found.append(front)
+        return found
+
+    def product(values):
+        result = values[0]
+        for value in values[1:]:
+            result = result * value
+        return result
+
+    slabs = partners + [me]
+    slab_ranks = [rank[slab * outer_count + group] for slab in slabs]
+
+    @pl.loop(0, chunks)
+    def _(chunk):
+        for partner in partners:
+            receive(partner, chunk).wait_recv()
+        rows = rows_of(chunk)
+        for column in range(0, width, 128):
+            columns = slice(column, column + 128)
+
+            def value(slab, k):
+                source = pieces if slab is me else arrived
+                return source[slab, k, rows, columns]
+
+            clear = [value(slab, 3) for slab in slabs]
+            weights = fronts(clear, slab_ranks)
+            for k in range(3):
+                banded[k, rows, columns] = sum(
+                    weights[i] * value(slab, k) for i, slab in enumerate(slabs)
+                )
+            banded[3, rows, columns] = product(clear)
+        for partner in outer_partners:
+            outer_copy(partner, group, chunk).start()
+
+    ordered = outer_partners + [group]
+    group_ranks = [rank[g] for g in ordered]
+    mine = pl.ds(pl.multiple_of(group * part, 128), part)
+
+    @pl.loop(0, chunks)
+    def _(chunk):
+        for partner in outer_partners:
+            outer_copy(group, partner, chunk).wait_recv()
+        rows = rows_of(chunk)
+
+        def value(g, k):
+            if g is group:
+                return banded[k, rows, mine]
+            return groups[g, k, rows, :]
+
+        clear = [value(g, 3) for g in ordered]
+        weights = fronts(clear, group_ranks)
+        for k in range(3):
+            out[k, rows, :] = sum(weights[i] * value(g, k) for i, g in enumerate(ordered))
+        out[3, rows, :] = 1.0 - product(clear)
+
+    @pl.loop(0, chunks)
+    def _(chunk):
+        for partner in partners:
+            send(partner, chunk).wait_send()
+        for partner in outer_partners:
+            outer_copy(partner, group, chunk).wait_send()
+
+
+def fused(density, extinction, occupancy, colour_slope, slab_rank):
+    inner_count = lax.axis_size("inner")
+    outer_count = lax.axis_size("outer")
+    slices, height, width = density.shape
+    band, part = height // inner_count, width // outer_count
+    chunks = band // ROWS
+    vmem = pl.BlockSpec(memory_space=pltpu.VMEM)
+    smem = pl.BlockSpec(memory_space=pltpu.SMEM)
+    return pl.pallas_call(
+        functools.partial(fused_kernel, inner_count, outer_count),
+        out_shape=jax.ShapeDtypeStruct((4, band, part), jnp.float32),
+        in_specs=[pl.BlockSpec(memory_space=pl.ANY), smem, vmem, smem, smem],
+        out_specs=vmem,
+        scratch_shapes=[
+            pltpu.VMEM((slices, height, width), density.dtype),
+            pltpu.VMEM((occupancy.shape[1], width), jnp.float32),
+            pltpu.VMEM((inner_count, 4, band, width), jnp.float32),
+            pltpu.VMEM((inner_count, 4, band, width), jnp.float32),
+            pltpu.VMEM((4, band, width), jnp.float32),
+            pltpu.VMEM((outer_count, 4, band, part), jnp.float32),
+            pltpu.SemaphoreType.DMA((inner_count,)),
+            pltpu.SemaphoreType.DMA((inner_count, chunks)),
+            pltpu.SemaphoreType.DMA((inner_count, chunks)),
+            pltpu.SemaphoreType.DMA((outer_count, chunks)),
+            pltpu.SemaphoreType.DMA((outer_count, chunks)),
+        ],
+        compiler_params=pltpu.CompilerParams(
+            collective_id=0, has_side_effects=True, vmem_limit_bytes=40 * 2**20
+        ),
+    )(density, extinction, occupancy, colour_slope, slab_rank)
+
+
 def solution(mesh):
     placed = (
         P(("inner", "outer"), None, "tile"),
@@ -62,8 +299,15 @@
         P(),
         P(),
     )
+
+    def local(density, *rest):
+        part = density.shape[2] // mesh.shape["outer"]
+        band = density.shape[1] // mesh.shape["inner"]
+        whole = part % 128 == 0 and band % ROWS == 0 and mesh.shape["inner"] % 2 == 0
+        return (fused if whole else shards)(density, *rest)
+
     return jax.shard_map(
-        shards,
+        local,
         mesh=mesh,
         in_specs=placed,
         out_specs=P(None, "inner", ("tile", "outer")),

time: 174 us -> 38.1 us (0.22)
  other arithmetic: 71.8 us -> 0 us
  local copies, waits for them, and re-layouts: 43.3 us -> 5.55 us
  waiting for transfers between devices: 32.7 us -> 0 us
  Pallas kernels: 0 us -> 32.4 us
  loops' own time: 12.6 us -> 0 us
  starting transfers between devices: 8.05 us -> 0 us
  matrix products: 4.3 us -> 0 us
    all_to_all x2 -> x0, waiting for transfers between devices: 32.7 us -> none  [the longest x1 24.2 us: shards(): lax.all_to_all(pieces[None], 'inner', split_axis=2, concat_axis=0, tiled=...]
    pallas_call x0 -> x1, Pallas kernels: none -> 32.4 us  [fused(): pl.pallas_call(functools.partial(fused_kernel, inner_count, outer_count),...]
    mul x32 -> x0, other arithmetic: 32.2 us -> none  [the longest x16 31.2 us: advance(): through = through * (1.0 - opacity)]
    dynamic_slice x48 -> x0, local copies, waits for them, and re-layouts: 28.5 us -> none  [march(): lax.scan(advance, start, (density, extinction))]
    add x16 -> x0, other arithmetic: 15.3 us -> none  [advance(): colour_sum = colour_sum + (through * opacity)[None] * colour]
    another operation x2 -> x0, other arithmetic: 15 us -> none  [composite(): running = jnp.cumprod(ordered[:, 3], axis=0)]
    another operation x1 -> x0, loops' own time: 12.6 us -> none  [march(): lax.scan(advance, start, (density, extinction))]
    all_to_all x2 -> x0, starting transfers between devices: 8.05 us -> none  [the longest x1 4.34 us: shards(): lax.all_to_all(pieces[None], 'inner', split_axis=2, concat_axis=0, tiled=...]
  transfers between devices with their start and end apart: 2 -> 0, of which waited for: 2 -> 0; matrix products, arithmetic and copies ran while one was open for 1% -> 0% of each run, Pallas kernels for 0% -> 0%
where the time goes in v1:
time: 38.1 us; the launch traced here: 37.9 us
  Pallas kernels  32.4 us (85%)
  local copies, waits for them, and re-layouts  5.55 us (15%)
    pallas_call x1, Pallas kernels, fused(): pl.pallas_call(functools.partial(fused_kernel, inner_count, outer_count),...  32.4 us
    unnamed x11, local copies, waits for them, and re-layouts  5.55 us

profile of v1, /device:TPU:0, one launch (start us, length us, event | category | flops | bytes accessed | tf_op | source)
XLA Modules:
  0.0 37.9 jit_solution(2402323303695733191)
XLA Ops:
  0.0 0.0 copy-start
  0.0 2.2 %copy-done = bf16[16,256,512]{2,1,0:T(8,128)(2,1)S(1)} copy-done((bf16[16,256,512]{2,1,0:T(8,128)(2,1)S(1)}, bf16[16,256,512]{2,1,0:T(8,128)(2,1)}, u32[]{:S(2)}) %copy-start) | copy-done | bytes 4194328
  2.2 0.0 copy-start.1
  2.2 0.7 %copy-done.1 = s32[1,16,32]{2,1,0:T(8,128)S(1)} copy-done((s32[1,16,32]{2,1,0:T(8,128)S(1)}, s32[1,16,32]{2,1,0:T(8,128)}, u32[]{:S(2)}) %copy-start.1) | copy-done | bytes 2072
  2.9 0.0 copy-start.2
  2.9 0.7 %copy-done.2 = f32[16]{0:T(128)S(1)} copy-done((f32[16]{0:T(128)S(1)}, f32[16]{0:T(128)}, u32[]{:S(2)}) %copy-start.2) | copy-done | bytes 88
  3.5 0.0 copy-start.3
  3.5 0.7 %copy-done.3 = f32[3]{0:T(128)S(1)} copy-done((f32[3]{0:T(128)S(1)}, f32[3]{0:T(128)}, u32[]{:S(2)}) %copy-start.3) | copy-done | bytes 36
  4.2 0.0 copy-start.4
  4.2 0.7 %copy-done.4 = s32[8]{0:T(128)S(1)} copy-done((s32[8]{0:T(128)S(1)}, s32[8]{0:T(128)}, u32[]{:S(2)}) %copy-start.4) | copy-done | bytes 56
  4.9 32.4 %shard_map.55 = f32[4,64,256]{2,1,0:T(8,128)S(1)} custom-call(bf16[16,256,512]{2,1,0:T(8,128)(2,1)S(1)} %copy-done, f32[16]{0:T(128)S(1)} %copy-done.2, s32[1,16,32]{2,1,0:T(8,128)S(1)} %copy-done.1, f32[3]{0:T(128)S(1)} %copy-done.3, s32[8]{0:T(128)S(1)} %copy-done.4), custom_call_target="tpu_custom_call" | custom-call | tf_op jit(solution)/shard_map/pallas_call | solution.py:270
  37.2 0.7 %copy.7 = f32[4,64,256]{2,1,0:T(8,128)} copy(f32[4,64,256]{2,1,0:T(8,128)S(1)} %shard_map.55) | data formatting | bytes 524288
Async XLA Ops:
  0.0 2.2 %copy-start = (bf16[16,256,512]{2,1,0:T(8,128)(2,1)S(1)}, bf16[16,256,512]{2,1,0:T(8,128)(2,1)}, u32[]{:S(2)}) copy-start(bf16[16,256,512]{2,1,0:T(8,128)(2,1)} %density.1) | copy-start | bytes 12582916
  2.2 0.7 %copy-start.1 = (s32[1,16,32]{2,1,0:T(8,128)S(1)}, s32[1,16,32]{2,1,0:T(8,128)}, u32[]{:S(2)}) copy-start(s32[1,16,32]{2,1,0:T(8,128)} %occupancy.1) | copy-start | bytes 6148
  2.9 0.7 %copy-start.2 = (f32[16]{0:T(128)S(1)}, f32[16]{0:T(128)}, u32[]{:S(2)}) copy-start(f32[16]{0:T(128)} %extinction.1) | copy-start | bytes 196
  3.5 0.7 %copy-start.3 = (f32[3]{0:T(128)S(1)}, f32[3]{0:T(128)}, u32[]{:S(2)}) copy-start(f32[3]{0:T(128)} %slope.1) | copy-start | bytes 40
  4.2 0.7 %copy-start.4 = (s32[8]{0:T(128)S(1)}, s32[8]{0:T(128)}, u32[]{:S(2)}) copy-start(s32[8]{0:T(128)} %rank.1) | copy-start | bytes 100

commit v2 on v1

--- a/solution.py
+++ b/solution.py
@@ -65,9 +65,10 @@
 
 def fused_kernel(
     inner_count, outer_count,
-    density, extinction, occupancy, slope, rank, out,
+    density, extinction_in, occupancy_in, slope_in, rank_in, out,
+    extinction, occupancy, slope, rank,
     field, fill, pieces, arrived, banded, groups,
-    load_sem, send_sem, recv_sem, outer_send_sem, outer_recv_sem,
+    small_sem, load_sem, send_sem, recv_sem, outer_send_sem, outer_recv_sem,
 ):
     slices, height, width = field.shape
     band = height // inner_count
@@ -91,6 +92,15 @@
             density.at[:, rows, :], field.at[:, rows, :], load_sem.at[owner]
         )
 
+    small = [
+        pltpu.make_async_copy(source, target, small_sem.at[index])
+        for index, (source, target) in enumerate([
+            (extinction_in, extinction), (occupancy_in, occupancy),
+            (slope_in, slope), (rank_in, rank),
+        ])
+    ]
+    for copy in small:
+        copy.start()
     for owner in partners + [me]:
         load(owner).start()
 
@@ -99,6 +109,9 @@
         pl.semaphore_signal(barrier, inc=1, device_id={"inner": partner}, device_id_type=MESH)
     for partner in outer_partners:
         pl.semaphore_signal(barrier, inc=1, device_id={"outer": partner}, device_id_type=MESH)
+
+    for copy in small:
+        copy.wait()
 
     block_rows, block_columns = occupancy.shape[1:]
     spread = (
@@ -266,19 +279,23 @@
     band, part = height // inner_count, width // outer_count
     chunks = band // ROWS
     vmem = pl.BlockSpec(memory_space=pltpu.VMEM)
-    smem = pl.BlockSpec(memory_space=pltpu.SMEM)
     return pl.pallas_call(
         functools.partial(fused_kernel, inner_count, outer_count),
         out_shape=jax.ShapeDtypeStruct((4, band, part), jnp.float32),
-        in_specs=[pl.BlockSpec(memory_space=pl.ANY), smem, vmem, smem, smem],
+        in_specs=[pl.BlockSpec(memory_space=pl.ANY)] * 5,
         out_specs=vmem,
         scratch_shapes=[
+            pltpu.SMEM(extinction.shape, extinction.dtype),
+            pltpu.VMEM(occupancy.shape, occupancy.dtype),
+            pltpu.SMEM(colour_slope.shape, colour_slope.dtype),
+            pltpu.SMEM(slab_rank.shape, slab_rank.dtype),
             pltpu.VMEM((slices, height, width), density.dtype),
             pltpu.VMEM((occupancy.shape[1], width), jnp.float32),
             pltpu.VMEM((inner_count, 4, band, width), jnp.float32),
             pltpu.VMEM((inner_count, 4, band, width), jnp.float32),
             pltpu.VMEM((4, band, width), jnp.float32),
             pltpu.VMEM((outer_count, 4, band, part), jnp.float32),
+            pltpu.SemaphoreType.DMA((4,)),
             pltpu.SemaphoreType.DMA((inner_count,)),
             pltpu.SemaphoreType.DMA((inner_count, chunks)),
             pltpu.SemaphoreType.DMA((inner_count, chunks)),
@@ -286,7 +303,7 @@
             pltpu.SemaphoreType.DMA((outer_count, chunks)),
         ],
         compiler_params=pltpu.CompilerParams(
-            collective_id=0, has_side_effects=True, vmem_limit_bytes=40 * 2**20
+            collective_id=0, has_side_effects=True, vmem_limit_bytes=60 * 2**20
         ),
     )(density, extinction, occupancy, colour_slope, slab_rank)
 

time: 38.1 us -> 34.7 us (0.911)
  local copies, waits for them, and re-layouts: 5.55 us -> 1.67 us
  Pallas kernels: 32.4 us -> 32.9 us
    unnamed x11 -> x1, local copies, waits for them, and re-layouts: 5.55 us -> 1.67 us
    pallas_call x1, Pallas kernels: 32.4 us -> 32.9 us  [fused(): pl.pallas_call(functools.partial(fused_kernel, inner_count, outer_count),...]
where the time goes in v2:
time: 34.7 us; the launch traced here: 34.6 us
  Pallas kernels  32.9 us (95%)
  local copies, waits for them, and re-layouts  1.67 us (5%)
    pallas_call x1, Pallas kernels, fused(): pl.pallas_call(functools.partial(fused_kernel, inner_count, outer_count),...  32.9 us
    unnamed x1, local copies, waits for them, and re-layouts  1.67 us

profile of v2, /device:TPU:0, one launch (start us, length us, event | category | flops | bytes accessed | tf_op | source)
XLA Modules:
  0.0 34.6 jit_solution(15432979222937501085)
XLA Ops:
  0.0 32.9 %shard_map.55 = f32[4,64,256]{2,1,0:T(8,128)} custom-call(bf16[16,256,512]{2,1,0:T(8,128)(2,1)} %density.1, f32[16]{0:T(128)} %extinction_in.1, s32[1,16,32]{2,1,0:T(8,128)} %occupancy_in.1, f32[3]{0:T(128)} %slope_in.1, s32[8]{0:T(128)} %rank_in.1), custom_call_target="tpu_custom_call" | custom-call | tf_op jit(solution)/shard_map/pallas_call | solution.py:282
  32.9 1.7 %copy.7 = f32[4,64,256]{2,1,0:T(8,128)} copy(f32[4,64,256]{2,1,0:T(8,128)} %shard_map.55) | data formatting | bytes 524288

commit v3 on v2

--- a/solution.py
+++ b/solution.py
@@ -67,8 +67,9 @@
     inner_count, outer_count,
     density, extinction_in, occupancy_in, slope_in, rank_in, out,
     extinction, occupancy, slope, rank,
-    field, fill, pieces, arrived, banded, groups,
-    small_sem, load_sem, send_sem, recv_sem, outer_send_sem, outer_recv_sem,
+    field, fill, pieces, near, between_out, between, pair_out, pair, banded, groups,
+    small_sem, load_sem, near_send, near_recv, between_send, between_recv,
+    pair_send, pair_recv, outer_send, outer_recv,
 ):
     slices, height, width = field.shape
     band = height // inner_count
@@ -77,19 +78,16 @@
     me = lax.axis_index("inner")
     group = lax.axis_index("outer")
 
-    pairs = inner_count // 2
     chip, core = me // 2, me % 2
-    partners = []
-    for step in range(1, pairs):
-        other = lax.rem(chip + step, pairs)
-        partners += [other * 2 + core, other * 2 + (1 - core)]
-    partners.append(chip * 2 + (1 - core))
+    sibling = chip * 2 + (1 - core)
+    across = (1 - chip) * 2 + core
+    diagonal = (1 - chip) * 2 + (1 - core)
     outer_partners = [lax.rem(group + step, outer_count) for step in range(1, outer_count)]
 
-    def load(owner):
-        rows = pl.ds(pl.multiple_of(owner * band, ROWS), band)
+    def load(owner, chunk):
+        rows = pl.ds(pl.multiple_of(owner * band + chunk * ROWS, ROWS), ROWS)
         return pltpu.make_async_copy(
-            density.at[:, rows, :], field.at[:, rows, :], load_sem.at[owner]
+            density.at[:, rows, :], field.at[:, rows, :], load_sem.at[owner, chunk]
         )
 
     small = [
@@ -101,15 +99,15 @@
     ]
     for copy in small:
         copy.start()
-    for owner in partners + [me]:
-        load(owner).start()
+    for chunk in range(chunks):
+        for owner in (sibling, me, diagonal, across):
+            load(owner, chunk).start()
 
     barrier = pltpu.get_barrier_semaphore()
-    for partner in partners:
+    for partner in (sibling, across):
         pl.semaphore_signal(barrier, inc=1, device_id={"inner": partner}, device_id_type=MESH)
     for partner in outer_partners:
         pl.semaphore_signal(barrier, inc=1, device_id={"outer": partner}, device_id_type=MESH)
-
     for copy in small:
         copy.wait()
 
@@ -126,6 +124,7 @@
     block_height = height // block_rows
 
     def march(owner, chunk):
+        load(owner, chunk).wait()
         start = pl.multiple_of(owner * band + chunk * ROWS, ROWS)
         to = pl.ds(pl.multiple_of(chunk * ROWS, ROWS), ROWS)
         for column in range(0, width, COLS):
@@ -149,99 +148,114 @@
     def rows_of(chunk):
         return pl.ds(pl.multiple_of(chunk * ROWS, ROWS), ROWS)
 
-    def send(partner, chunk):
+    def copy_near(slot, chunk):
         return pltpu.make_async_remote_copy(
-            src_ref=pieces.at[partner, :, rows_of(chunk), :],
-            dst_ref=arrived.at[me, :, rows_of(chunk), :],
-            send_sem=send_sem.at[partner, chunk],
-            recv_sem=recv_sem.at[me, chunk],
-            device_id={"inner": partner},
+            src_ref=pieces.at[(sibling, diagonal)[slot], :, rows_of(chunk), :],
+            dst_ref=near.at[slot, :, rows_of(chunk), :],
+            send_sem=near_send.at[slot, chunk],
+            recv_sem=near_recv.at[slot, chunk],
+            device_id={"inner": sibling},
             device_id_type=MESH,
         )
 
-    def receive(partner, chunk):
+    def copy_between(chunk):
         return pltpu.make_async_remote_copy(
-            src_ref=pieces.at[partner, :, rows_of(chunk), :],
-            dst_ref=arrived.at[partner, :, rows_of(chunk), :],
-            send_sem=send_sem.at[partner, chunk],
-            recv_sem=recv_sem.at[partner, chunk],
-            device_id={"inner": partner},
+            src_ref=between_out.at[rows_of(chunk), :],
+            dst_ref=between.at[rows_of(chunk), :],
+            send_sem=between_send.at[chunk],
+            recv_sem=between_recv.at[chunk],
+            device_id={"inner": across},
             device_id_type=MESH,
         )
 
-    def outer_copy(partner, slot, chunk):
+    def copy_pair(chunk):
+        return pltpu.make_async_remote_copy(
+            src_ref=pair_out.at[:, rows_of(chunk), :],
+            dst_ref=pair.at[:, rows_of(chunk), :],
+            send_sem=pair_send.at[chunk],
+            recv_sem=pair_recv.at[chunk],
+            device_id={"inner": across},
+            device_id_type=MESH,
+        )
+
+    def copy_outer(partner, slot, chunk):
         return pltpu.make_async_remote_copy(
             src_ref=banded.at[:, rows_of(chunk), pl.ds(pl.multiple_of(partner * part, 128), part)],
             dst_ref=groups.at[slot, :, rows_of(chunk), :],
-            send_sem=outer_send_sem.at[partner, chunk],
-            recv_sem=outer_recv_sem.at[slot, chunk],
+            send_sem=outer_send.at[partner, chunk],
+            recv_sem=outer_recv.at[slot, chunk],
             device_id={"outer": partner},
             device_id_type=MESH,
         )
 
-    far = partners[:-1]
-    near = partners[-1]
-    for index, owner in enumerate(far):
-        load(owner).wait()
-        if index == 0:
-            pl.semaphore_wait(barrier, len(partners) + len(outer_partners))
+    def rank_of(slab):
+        return rank[slab * outer_count + group]
+
+    mine_rank, near_rank = rank_of(me), rank_of(sibling)
+    own_first = mine_rank < near_rank
+    far_low = jnp.minimum(rank_of(across), rank_of(diagonal))
+    far_high = jnp.maximum(rank_of(across), rank_of(diagonal))
+    tiles = [slice(column, column + 128) for column in range(0, width, 128)]
+
+    def inside(value):
+        return (far_low < value) & (value < far_high)
+
+    pl.semaphore_wait(barrier, 2 + len(outer_partners))
 
     @pl.loop(0, chunks)
     def _(chunk):
-        for owner in far:
-            march(owner, chunk)
-            send(owner, chunk).start()
-
-    load(near).wait()
-    load(me).wait()
+        rows = rows_of(chunk)
+        march(sibling, chunk)
+        copy_near(0, chunk).start()
+        march(me, chunk)
+        copy_near(0, chunk).wait_recv()
+        for columns in tiles:
+            between_out[rows, columns] = jnp.where(
+                inside(mine_rank), pieces[me, 3, rows, columns], 1.0
+            ) * jnp.where(inside(near_rank), near[0, 3, rows, columns], 1.0)
+        copy_between(chunk).start()
+        march(diagonal, chunk)
+        copy_near(1, chunk).start()
+        march(across, chunk)
+        copy_near(1, chunk).wait_recv()
+        copy_between(chunk).wait_recv()
+        for columns in tiles:
+            own = [pieces[across, k, rows, columns] for k in range(4)]
+            other = [near[1, k, rows, columns] for k in range(4)]
+            first = jnp.where(own_first, own[3], other[3])
+            front = first * between[rows, columns]
+            for k in range(3):
+                pair_out[k, rows, columns] = jnp.where(
+                    own_first, own[k] + front * other[k], other[k] + front * own[k]
+                )
+            pair_out[3, rows, columns] = first
+            pair_out[4, rows, columns] = own[3] * other[3]
+        copy_pair(chunk).start()
 
     @pl.loop(0, chunks)
     def _(chunk):
-        march(near, chunk)
-        send(near, chunk).start()
-        march(me, chunk)
-
-    def fronts(values, ranks):
-        found = []
-        for k in range(len(values)):
-            front = None
-            for j in range(len(values)):
-                if j != k:
-                    factor = jnp.where(ranks[j] < ranks[k], values[j], 1.0)
-                    front = factor if front is None else front * factor
-            found.append(front)
-        return found
-
-    def product(values):
-        result = values[0]
-        for value in values[1:]:
-            result = result * value
-        return result
-
-    slabs = partners + [me]
-    slab_ranks = [rank[slab * outer_count + group] for slab in slabs]
-
-    @pl.loop(0, chunks)
-    def _(chunk):
-        for partner in partners:
-            receive(partner, chunk).wait_recv()
+        copy_pair(chunk).wait_recv()
         rows = rows_of(chunk)
-        for column in range(0, width, 128):
-            columns = slice(column, column + 128)
-
-            def value(slab, k):
-                source = pieces if slab is me else arrived
-                return source[slab, k, rows, columns]
-
-            clear = [value(slab, 3) for slab in slabs]
-            weights = fronts(clear, slab_ranks)
+        for columns in tiles:
+            own = [pieces[me, k, rows, columns] for k in range(4)]
+            other = [near[0, k, rows, columns] for k in range(4)]
+            far = [pair[k, rows, columns] for k in range(5)]
+
+            def behind_far(value):
+                return jnp.where(far_high < value, far[4], jnp.where(far_low < value, far[3], 1.0))
+
+            own_front = behind_far(mine_rank) * jnp.where(own_first, 1.0, other[3])
+            other_front = behind_far(near_rank) * jnp.where(own_first, own[3], 1.0)
+            far_front = jnp.where(mine_rank < far_low, own[3], 1.0) * jnp.where(
+                near_rank < far_low, other[3], 1.0
+            )
             for k in range(3):
-                banded[k, rows, columns] = sum(
-                    weights[i] * value(slab, k) for i, slab in enumerate(slabs)
+                banded[k, rows, columns] = (
+                    own_front * own[k] + other_front * other[k] + far_front * far[k]
                 )
-            banded[3, rows, columns] = product(clear)
+            banded[3, rows, columns] = own[3] * other[3] * far[4]
         for partner in outer_partners:
-            outer_copy(partner, group, chunk).start()
+            copy_outer(partner, group, chunk).start()
 
     ordered = outer_partners + [group]
     group_ranks = [rank[g] for g in ordered]
@@ -250,7 +264,7 @@
     @pl.loop(0, chunks)
     def _(chunk):
         for partner in outer_partners:
-            outer_copy(group, partner, chunk).wait_recv()
+            copy_outer(group, partner, chunk).wait_recv()
         rows = rows_of(chunk)
 
         def value(g, k):
@@ -259,17 +273,28 @@
             return groups[g, k, rows, :]
 
         clear = [value(g, 3) for g in ordered]
-        weights = fronts(clear, group_ranks)
+        total = [0.0, 0.0, 0.0]
+        for i, g in enumerate(ordered):
+            front = 1.0
+            for j in range(len(ordered)):
+                if j != i:
+                    front = front * jnp.where(group_ranks[j] < group_ranks[i], clear[j], 1.0)
+            total = [total[k] + front * value(g, k) for k in range(3)]
         for k in range(3):
-            out[k, rows, :] = sum(weights[i] * value(g, k) for i, g in enumerate(ordered))
-        out[3, rows, :] = 1.0 - product(clear)
+            out[k, rows, :] = total[k]
+        through = clear[0]
+        for other in clear[1:]:
+            through = through * other
+        out[3, rows, :] = 1.0 - through
 
     @pl.loop(0, chunks)
     def _(chunk):
-        for partner in partners:
-            send(partner, chunk).wait_send()
+        copy_near(0, chunk).wait_send()
+        copy_near(1, chunk).wait_send()
+        copy_between(chunk).wait_send()
+        copy_pair(chunk).wait_send()
         for partner in outer_partners:
-            outer_copy(partner, group, chunk).wait_send()
+            copy_outer(partner, group, chunk).wait_send()
 
 
 def fused(density, extinction, occupancy, colour_slope, slab_rank):
@@ -292,13 +317,21 @@
             pltpu.VMEM((slices, height, width), density.dtype),
             pltpu.VMEM((occupancy.shape[1], width), jnp.float32),
             pltpu.VMEM((inner_count, 4, band, width), jnp.float32),
-            pltpu.VMEM((inner_count, 4, band, width), jnp.float32),
+            pltpu.VMEM((2, 4, band, width), jnp.float32),
+            pltpu.VMEM((band, width), jnp.float32),
+            pltpu.VMEM((band, width), jnp.float32),
+            pltpu.VMEM((5, band, width), jnp.float32),
+            pltpu.VMEM((5, band, width), jnp.float32),
             pltpu.VMEM((4, band, width), jnp.float32),
             pltpu.VMEM((outer_count, 4, band, part), jnp.float32),
             pltpu.SemaphoreType.DMA((4,)),
-            pltpu.SemaphoreType.DMA((inner_count,)),
             pltpu.SemaphoreType.DMA((inner_count, chunks)),
-            pltpu.SemaphoreType.DMA((inner_count, chunks)),
+            pltpu.SemaphoreType.DMA((2, chunks)),
+            pltpu.SemaphoreType.DMA((2, chunks)),
+            pltpu.SemaphoreType.DMA((chunks,)),
+            pltpu.SemaphoreType.DMA((chunks,)),
+            pltpu.SemaphoreType.DMA((chunks,)),
+            pltpu.SemaphoreType.DMA((chunks,)),
             pltpu.SemaphoreType.DMA((outer_count, chunks)),
             pltpu.SemaphoreType.DMA((outer_count, chunks)),
         ],
@@ -320,7 +353,7 @@
     def local(density, *rest):
         part = density.shape[2] // mesh.shape["outer"]
         band = density.shape[1] // mesh.shape["inner"]
-        whole = part % 128 == 0 and band % ROWS == 0 and mesh.shape["inner"] % 2 == 0
+        whole = part % 128 == 0 and band % ROWS == 0 and mesh.shape["inner"] == 4
         return (fused if whole else shards)(density, *rest)
 
     return jax.shard_map(

time: 34.7 us -> 36.8 us (1.061)
  Pallas kernels: 32.9 us -> 35 us
    pallas_call x1, Pallas kernels: 32.9 us -> 35 us  [fused(): pl.pallas_call(functools.partial(fused_kernel, inner_count, outer_count),...]
where the time goes in v3:
time: 36.8 us; the launch traced here: 36.7 us
  Pallas kernels  35 us (95%)
  local copies, waits for them, and re-layouts  1.67 us (5%)
    pallas_call x1, Pallas kernels, fused(): pl.pallas_call(functools.partial(fused_kernel, inner_count, outer_count),...  35 us
    unnamed x1, local copies, waits for them, and re-layouts  1.67 us

profile of v3, /device:TPU:0, one launch (start us, length us, event | category | flops | bytes accessed | tf_op | source)
XLA Modules:
  0.0 36.7 jit_solution(13289027438236732587)
XLA Ops:
  0.0 35.0 %shard_map.55 = f32[4,64,256]{2,1,0:T(8,128)} custom-call(bf16[16,256,512]{2,1,0:T(8,128)(2,1)} %density.1, f32[16]{0:T(128)} %extinction_in.1, s32[1,16,32]{2,1,0:T(8,128)} %occupancy_in.1, f32[3]{0:T(128)} %slope_in.1, s32[8]{0:T(128)} %rank_in.1), custom_call_target="tpu_custom_call" | custom-call | tf_op jit(solution)/shard_map/pallas_call | solution.py:307
  35.0 1.7 %copy.7 = f32[4,64,256]{2,1,0:T(8,128)} copy(f32[4,64,256]{2,1,0:T(8,128)} %shard_map.55) | data formatting | bytes 524288

commit v4 on v3

--- a/solution.py
+++ b/solution.py
@@ -99,9 +99,10 @@
     ]
     for copy in small:
         copy.start()
-    for chunk in range(chunks):
-        for owner in (sibling, me, diagonal, across):
-            load(owner, chunk).start()
+    for owners in ((sibling, me), (diagonal, across)):
+        for chunk in range(chunks):
+            for owner in owners:
+                load(owner, chunk).start()
 
     barrier = pltpu.get_barrier_semaphore()
     for partner in (sibling, across):
@@ -202,23 +203,19 @@
 
     pl.semaphore_wait(barrier, 2 + len(outer_partners))
 
-    @pl.loop(0, chunks)
-    def _(chunk):
+    def open_between(chunk):
+        copy_near(0, chunk).wait_recv()
         rows = rows_of(chunk)
-        march(sibling, chunk)
-        copy_near(0, chunk).start()
-        march(me, chunk)
-        copy_near(0, chunk).wait_recv()
         for columns in tiles:
             between_out[rows, columns] = jnp.where(
                 inside(mine_rank), pieces[me, 3, rows, columns], 1.0
             ) * jnp.where(inside(near_rank), near[0, 3, rows, columns], 1.0)
         copy_between(chunk).start()
-        march(diagonal, chunk)
-        copy_near(1, chunk).start()
-        march(across, chunk)
+
+    def merge_pair(chunk):
         copy_near(1, chunk).wait_recv()
         copy_between(chunk).wait_recv()
+        rows = rows_of(chunk)
         for columns in tiles:
             own = [pieces[across, k, rows, columns] for k in range(4)]
             other = [near[1, k, rows, columns] for k in range(4)]
@@ -231,6 +228,30 @@
             pair_out[3, rows, columns] = first
             pair_out[4, rows, columns] = own[3] * other[3]
         copy_pair(chunk).start()
+
+    @pl.loop(0, chunks + 1)
+    def _(chunk):
+        @pl.when(chunk < chunks)
+        def _():
+            march(sibling, chunk)
+            copy_near(0, chunk).start()
+            march(me, chunk)
+
+        @pl.when(chunk >= 1)
+        def _():
+            open_between(chunk - 1)
+
+    @pl.loop(0, chunks + 1)
+    def _(chunk):
+        @pl.when(chunk < chunks)
+        def _():
+            march(diagonal, chunk)
+            copy_near(1, chunk).start()
+            march(across, chunk)
+
+        @pl.when(chunk >= 1)
+        def _():
+            merge_pair(chunk - 1)
 
     @pl.loop(0, chunks)
     def _(chunk):

time: 36.8 us -> 32.2 us (0.88)
  Pallas kernels: 35 us -> 30.4 us
    pallas_call x1, Pallas kernels: 35 us -> 30.4 us  [fused(): pl.pallas_call(functools.partial(fused_kernel, inner_count, outer_count),...]
where the time goes in v4:
time: 32.2 us; the launch traced here: 32 us
  Pallas kernels  30.4 us (94%)
  local copies, waits for them, and re-layouts  1.67 us (5%)
    pallas_call x1, Pallas kernels, fused(): pl.pallas_call(functools.partial(fused_kernel, inner_count, outer_count),...  30.4 us
    unnamed x1, local copies, waits for them, and re-layouts  1.67 us

profile of v4, /device:TPU:0, one launch (start us, length us, event | category | flops | bytes accessed | tf_op | source)
XLA Modules:
  0.0 32.0 jit_solution(80050824840589757)
XLA Ops:
  0.0 30.4 %shard_map.55 = f32[4,64,256]{2,1,0:T(8,128)} custom-call(bf16[16,256,512]{2,1,0:T(8,128)(2,1)} %density.1, f32[16]{0:T(128)} %extinction_in.1, s32[1,16,32]{2,1,0:T(8,128)} %occupancy_in.1, f32[3]{0:T(128)} %slope_in.1, s32[8]{0:T(128)} %rank_in.1), custom_call_target="tpu_custom_call" | custom-call | tf_op jit(solution)/shard_map/pallas_call | solution.py:328
  30.4 1.7 %copy.7 = f32[4,64,256]{2,1,0:T(8,128)} copy(f32[4,64,256]{2,1,0:T(8,128)} %shard_map.55) | data formatting | bytes 524288

commit v5 on v4

--- a/solution.py
+++ b/solution.py
@@ -59,6 +59,7 @@
 
 
 ROWS = 16
+PIECE = 8
 COLS = 256
 MESH = pl.DeviceIdType.MESH
 
@@ -67,14 +68,15 @@
     inner_count, outer_count,
     density, extinction_in, occupancy_in, slope_in, rank_in, out,
     extinction, occupancy, slope, rank,
-    field, fill, pieces, near, between_out, between, pair_out, pair, banded, groups,
-    small_sem, load_sem, near_send, near_recv, between_send, between_recv,
+    field, fill, pieces, raw, near, between_out, between, pair_out, pair, banded, groups,
+    small_sem, load_sem, raw_send, raw_recv, near_send, near_recv, between_send, between_recv,
     pair_send, pair_recv, outer_send, outer_recv,
 ):
     slices, height, width = field.shape
     band = height // inner_count
     chunks = band // ROWS
     part = width // outer_count
+    per_chunk = ROWS // PIECE
     me = lax.axis_index("inner")
     group = lax.axis_index("outer")
 
@@ -99,13 +101,14 @@
     ]
     for copy in small:
         copy.start()
-    for owners in ((sibling, me), (diagonal, across)):
-        for chunk in range(chunks):
-            for owner in owners:
-                load(owner, chunk).start()
+    order = [(owner, 0) for owner in (across, diagonal)]
+    order += [(owner, chunk) for chunk in range(chunks) for owner in (sibling, me)]
+    order += [(owner, chunk) for chunk in range(1, chunks) for owner in (diagonal, across)]
+    for owner, chunk in order:
+        load(owner, chunk).start()
 
     barrier = pltpu.get_barrier_semaphore()
-    for partner in (sibling, across):
+    for partner in (sibling, across, diagonal):
         pl.semaphore_signal(barrier, inc=1, device_id={"inner": partner}, device_id_type=MESH)
     for partner in outer_partners:
         pl.semaphore_signal(barrier, inc=1, device_id={"outer": partner}, device_id_type=MESH)
@@ -149,6 +152,20 @@
     def rows_of(chunk):
         return pl.ds(pl.multiple_of(chunk * ROWS, ROWS), ROWS)
 
+    def piece_rows(piece):
+        return pl.ds(pl.multiple_of(piece * PIECE, PIECE), PIECE)
+
+    def copy_raw(slot):
+        partner = (across, diagonal)[slot]
+        return pltpu.make_async_remote_copy(
+            src_ref=pieces.at[partner, :, rows_of(0), :],
+            dst_ref=raw.at[slot],
+            send_sem=raw_send.at[slot],
+            recv_sem=raw_recv.at[slot],
+            device_id={"inner": partner},
+            device_id_type=MESH,
+        )
+
     def copy_near(slot, chunk):
         return pltpu.make_async_remote_copy(
             src_ref=pieces.at[(sibling, diagonal)[slot], :, rows_of(chunk), :],
@@ -169,22 +186,23 @@
             device_id_type=MESH,
         )
 
-    def copy_pair(chunk):
+    def copy_pair(piece):
         return pltpu.make_async_remote_copy(
-            src_ref=pair_out.at[:, rows_of(chunk), :],
-            dst_ref=pair.at[:, rows_of(chunk), :],
-            send_sem=pair_send.at[chunk],
-            recv_sem=pair_recv.at[chunk],
+            src_ref=pair_out.at[:, piece_rows(piece), :],
+            dst_ref=pair.at[:, piece_rows(piece), :],
+            send_sem=pair_send.at[piece],
+            recv_sem=pair_recv.at[piece],
             device_id={"inner": across},
             device_id_type=MESH,
         )
 
-    def copy_outer(partner, slot, chunk):
+    def copy_outer(partner, slot, piece):
+        columns = pl.ds(pl.multiple_of(partner * part, 128), part)
         return pltpu.make_async_remote_copy(
-            src_ref=banded.at[:, rows_of(chunk), pl.ds(pl.multiple_of(partner * part, 128), part)],
-            dst_ref=groups.at[slot, :, rows_of(chunk), :],
-            send_sem=outer_send.at[partner, chunk],
-            recv_sem=outer_recv.at[slot, chunk],
+            src_ref=banded.at[:, piece_rows(piece), columns],
+            dst_ref=groups.at[slot, :, piece_rows(piece), :],
+            send_sem=outer_send.at[partner, piece],
+            recv_sem=outer_recv.at[slot, piece],
             device_id={"outer": partner},
             device_id_type=MESH,
         )
@@ -201,7 +219,6 @@
     def inside(value):
         return (far_low < value) & (value < far_high)
 
-    pl.semaphore_wait(barrier, 2 + len(outer_partners))
 
     def open_between(chunk):
         copy_near(0, chunk).wait_recv()
@@ -227,7 +244,14 @@
                 )
             pair_out[3, rows, columns] = first
             pair_out[4, rows, columns] = own[3] * other[3]
-        copy_pair(chunk).start()
+        for piece in range(per_chunk):
+            copy_pair(chunk * per_chunk + piece).start()
+
+    march(across, 0)
+    march(diagonal, 0)
+    pl.semaphore_wait(barrier, 3 + len(outer_partners))
+    copy_raw(0).start()
+    copy_raw(1).start()
 
     @pl.loop(0, chunks + 1)
     def _(chunk):
@@ -237,11 +261,11 @@
             copy_near(0, chunk).start()
             march(me, chunk)
 
-        @pl.when(chunk >= 1)
+        @pl.when(chunk >= 2)
         def _():
             open_between(chunk - 1)
 
-    @pl.loop(0, chunks + 1)
+    @pl.loop(1, chunks + 1)
     def _(chunk):
         @pl.when(chunk < chunks)
         def _():
@@ -249,14 +273,32 @@
             copy_near(1, chunk).start()
             march(across, chunk)
 
-        @pl.when(chunk >= 1)
+        @pl.when(chunk >= 2)
         def _():
             merge_pair(chunk - 1)
 
-    @pl.loop(0, chunks)
-    def _(chunk):
-        copy_pair(chunk).wait_recv()
-        rows = rows_of(chunk)
+    def merge_raw():
+        copy_near(0, 0).wait_recv()
+        copy_raw(0).wait_recv()
+        copy_raw(1).wait_recv()
+        rows = rows_of(0)
+        across_first = rank_of(across) < rank_of(diagonal)
+        for columns in tiles:
+            one = [raw[0, k, :, columns] for k in range(4)]
+            other = [raw[1, k, :, columns] for k in range(4)]
+            first = jnp.where(across_first, one[3], other[3])
+            front = first * jnp.where(
+                inside(mine_rank), pieces[me, 3, rows, columns], 1.0
+            ) * jnp.where(inside(near_rank), near[0, 3, rows, columns], 1.0)
+            for k in range(3):
+                pair[k, rows, columns] = jnp.where(
+                    across_first, one[k] + front * other[k], other[k] + front * one[k]
+                )
+            pair[3, rows, columns] = first
+            pair[4, rows, columns] = one[3] * other[3]
+
+    def composite(piece):
+        rows = piece_rows(piece)
         for columns in tiles:
             own = [pieces[me, k, rows, columns] for k in range(4)]
             other = [near[0, k, rows, columns] for k in range(4)]
@@ -276,17 +318,28 @@
                 )
             banded[3, rows, columns] = own[3] * other[3] * far[4]
         for partner in outer_partners:
-            copy_outer(partner, group, chunk).start()
+            copy_outer(partner, group, piece).start()
+
+    merge_raw()
+
+    @pl.loop(0, per_chunk)
+    def _(piece):
+        composite(piece)
+
+    @pl.loop(per_chunk, chunks * per_chunk)
+    def _(piece):
+        copy_pair(piece).wait_recv()
+        composite(piece)
 
     ordered = outer_partners + [group]
     group_ranks = [rank[g] for g in ordered]
     mine = pl.ds(pl.multiple_of(group * part, 128), part)
 
-    @pl.loop(0, chunks)
-    def _(chunk):
+    @pl.loop(0, chunks * per_chunk)
+    def _(piece):
         for partner in outer_partners:
-            copy_outer(group, partner, chunk).wait_recv()
-        rows = rows_of(chunk)
+            copy_outer(group, partner, piece).wait_recv()
+        rows = piece_rows(piece)
 
         def value(g, k):
             if g is group:
@@ -308,14 +361,22 @@
             through = through * other
         out[3, rows, :] = 1.0 - through
 
-    @pl.loop(0, chunks)
+    copy_raw(0).wait_send()
+    copy_raw(1).wait_send()
+    copy_near(0, 0).wait_send()
+
+    @pl.loop(1, chunks)
     def _(chunk):
         copy_near(0, chunk).wait_send()
         copy_near(1, chunk).wait_send()
         copy_between(chunk).wait_send()
-        copy_pair(chunk).wait_send()
+        for piece in range(per_chunk):
+            copy_pair(chunk * per_chunk + piece).wait_send()
+
+    @pl.loop(0, chunks * per_chunk)
+    def _(piece):
         for partner in outer_partners:
-            copy_outer(partner, group, chunk).wait_send()
+            copy_outer(partner, group, piece).wait_send()
 
 
 def fused(density, extinction, occupancy, colour_slope, slab_rank):
@@ -338,6 +399,7 @@
             pltpu.VMEM((slices, height, width), density.dtype),
             pltpu.VMEM((occupancy.shape[1], width), jnp.float32),
             pltpu.VMEM((inner_count, 4, band, width), jnp.float32),
+            pltpu.VMEM((2, 4, ROWS, width), jnp.float32),
             pltpu.VMEM((2, 4, band, width), jnp.float32),
             pltpu.VMEM((band, width), jnp.float32),
             pltpu.VMEM((band, width), jnp.float32),
@@ -347,14 +409,16 @@
             pltpu.VMEM((outer_count, 4, band, part), jnp.float32),
             pltpu.SemaphoreType.DMA((4,)),
             pltpu.SemaphoreType.DMA((inner_count, chunks)),
+            pltpu.SemaphoreType.DMA((2,)),
+            pltpu.SemaphoreType.DMA((2,)),
             pltpu.SemaphoreType.DMA((2, chunks)),
             pltpu.SemaphoreType.DMA((2, chunks)),
             pltpu.SemaphoreType.DMA((chunks,)),
             pltpu.SemaphoreType.DMA((chunks,)),
-            pltpu.SemaphoreType.DMA((chunks,)),
-            pltpu.SemaphoreType.DMA((chunks,)),
-            pltpu.SemaphoreType.DMA((outer_count, chunks)),
-            pltpu.SemaphoreType.DMA((outer_count, chunks)),
+            pltpu.SemaphoreType.DMA((chunks * ROWS // PIECE,)),
+            pltpu.SemaphoreType.DMA((chunks * ROWS // PIECE,)),
+            pltpu.SemaphoreType.DMA((outer_count, chunks * ROWS // PIECE)),
+            pltpu.SemaphoreType.DMA((outer_count, chunks * ROWS // PIECE)),
         ],
         compiler_params=pltpu.CompilerParams(
             collective_id=0, has_side_effects=True, vmem_limit_bytes=60 * 2**20

time: 32.2 us -> 31.4 us (0.975)
  Pallas kernels: 30.4 us -> 29.6 us
    pallas_call x1, Pallas kernels: 30.4 us -> 29.6 us  [fused(): pl.pallas_call(functools.partial(fused_kernel, inner_count, outer_count),...]
where the time goes in v5:
time: 31.4 us; the launch traced here: 31.3 us
  Pallas kernels  29.6 us (94%)
  local copies, waits for them, and re-layouts  1.67 us (5%)
    pallas_call x1, Pallas kernels, fused(): pl.pallas_call(functools.partial(fused_kernel, inner_count, outer_count),...  29.6 us
    unnamed x1, local copies, waits for them, and re-layouts  1.67 us

profile of v5, /device:TPU:0, one launch (start us, length us, event | category | flops | bytes accessed | tf_op | source)
XLA Modules:
  0.0 31.3 jit_solution(3267477538008336784)
XLA Ops:
  0.0 29.6 %shard_map.55 = f32[4,64,256]{2,1,0:T(8,128)} custom-call(bf16[16,256,512]{2,1,0:T(8,128)(2,1)} %density.1, f32[16]{0:T(128)} %extinction_in.1, s32[1,16,32]{2,1,0:T(8,128)} %occupancy_in.1, f32[3]{0:T(128)} %slope_in.1, s32[8]{0:T(128)} %rank_in.1), custom_call_target="tpu_custom_call" | custom-call | tf_op jit(solution)/shard_map/pallas_call | solution.py:389
  29.6 1.7 %copy.7 = f32[4,64,256]{2,1,0:T(8,128)} copy(f32[4,64,256]{2,1,0:T(8,128)} %shard_map.55) | data formatting | bytes 524288

commit v6 on v5

--- a/solution.py
+++ b/solution.py
@@ -60,6 +60,7 @@
 
 ROWS = 16
 PIECE = 8
+LAG = 2
 COLS = 256
 MESH = pl.DeviceIdType.MESH
 
@@ -92,6 +93,11 @@
             density.at[:, rows, :], field.at[:, rows, :], load_sem.at[owner, chunk]
         )
 
+    barrier = pltpu.get_barrier_semaphore()
+    for partner in (sibling, across, diagonal):
+        pl.semaphore_signal(barrier, inc=1, device_id={"inner": partner}, device_id_type=MESH)
+    for partner in outer_partners:
+        pl.semaphore_signal(barrier, inc=1, device_id={"outer": partner}, device_id_type=MESH)
     small = [
         pltpu.make_async_copy(source, target, small_sem.at[index])
         for index, (source, target) in enumerate([
@@ -104,14 +110,9 @@
     order = [(owner, 0) for owner in (across, diagonal)]
     order += [(owner, chunk) for chunk in range(chunks) for owner in (sibling, me)]
     order += [(owner, chunk) for chunk in range(1, chunks) for owner in (diagonal, across)]
-    for owner, chunk in order:
+    for owner, chunk in order[:2]:
         load(owner, chunk).start()
 
-    barrier = pltpu.get_barrier_semaphore()
-    for partner in (sibling, across, diagonal):
-        pl.semaphore_signal(barrier, inc=1, device_id={"inner": partner}, device_id_type=MESH)
-    for partner in outer_partners:
-        pl.semaphore_signal(barrier, inc=1, device_id={"outer": partner}, device_id_type=MESH)
     for copy in small:
         copy.wait()
 
@@ -247,10 +248,12 @@
         for piece in range(per_chunk):
             copy_pair(chunk * per_chunk + piece).start()
 
+    for owner, chunk in order[2:]:
+        load(owner, chunk).start()
     march(across, 0)
-    march(diagonal, 0)
     pl.semaphore_wait(barrier, 3 + len(outer_partners))
     copy_raw(0).start()
+    march(diagonal, 0)
     copy_raw(1).start()
 
     @pl.loop(0, chunks + 1)
@@ -320,23 +323,11 @@
         for partner in outer_partners:
             copy_outer(partner, group, piece).start()
 
-    merge_raw()
-
-    @pl.loop(0, per_chunk)
-    def _(piece):
-        composite(piece)
-
-    @pl.loop(per_chunk, chunks * per_chunk)
-    def _(piece):
-        copy_pair(piece).wait_recv()
-        composite(piece)
-
     ordered = outer_partners + [group]
     group_ranks = [rank[g] for g in ordered]
     mine = pl.ds(pl.multiple_of(group * part, 128), part)
 
-    @pl.loop(0, chunks * per_chunk)
-    def _(piece):
+    def finish(piece):
         for partner in outer_partners:
             copy_outer(group, partner, piece).wait_recv()
         rows = piece_rows(piece)
@@ -360,6 +351,8 @@
         for other in clear[1:]:
             through = through * other
         out[3, rows, :] = 1.0 - through
+        for partner in outer_partners:
+            copy_outer(partner, group, piece).wait_send()
 
     copy_raw(0).wait_send()
     copy_raw(1).wait_send()
@@ -370,13 +363,23 @@
         copy_near(0, chunk).wait_send()
         copy_near(1, chunk).wait_send()
         copy_between(chunk).wait_send()
-        for piece in range(per_chunk):
-            copy_pair(chunk * per_chunk + piece).wait_send()
-
-    @pl.loop(0, chunks * per_chunk)
+
+    merge_raw()
+
+    @pl.loop(0, per_chunk)
     def _(piece):
-        for partner in outer_partners:
-            copy_outer(partner, group, piece).wait_send()
+        composite(piece)
+
+    @pl.loop(per_chunk, chunks * per_chunk)
+    def _(piece):
+        copy_pair(piece).wait_recv()
+        composite(piece)
+        copy_pair(piece).wait_send()
+        finish(piece - LAG)
+
+    @pl.loop(chunks * per_chunk - LAG, chunks * per_chunk)
+    def _(piece):
+        finish(piece)
 
 
 def fused(density, extinction, occupancy, colour_slope, slab_rank):

time: 31.4 us -> 30 us (0.955)
  Pallas kernels: 29.6 us -> 28.2 us
    pallas_call x1, Pallas kernels: 29.6 us -> 28.2 us  [fused(): pl.pallas_call(functools.partial(fused_kernel, inner_count, outer_count),...]
where the time goes in v6:
time: 30 us; the launch traced here: 29.9 us
  Pallas kernels  28.2 us (94%)
  local copies, waits for them, and re-layouts  1.67 us (6%)
    pallas_call x1, Pallas kernels, fused(): pl.pallas_call(functools.partial(fused_kernel, inner_count, outer_count),...  28.2 us
    unnamed x1, local copies, waits for them, and re-layouts  1.67 us

profile of v6, /device:TPU:0, one launch (start us, length us, event | category | flops | bytes accessed | tf_op | source)
XLA Modules:
  0.0 29.9 jit_solution(1948790499534635043)
XLA Ops:
  0.0 28.2 %shard_map.55 = f32[4,64,256]{2,1,0:T(8,128)} custom-call(bf16[16,256,512]{2,1,0:T(8,128)(2,1)} %density.1, f32[16]{0:T(128)} %extinction_in.1, s32[1,16,32]{2,1,0:T(8,128)} %occupancy_in.1, f32[3]{0:T(128)} %slope_in.1, s32[8]{0:T(128)} %rank_in.1), custom_call_target="tpu_custom_call" | custom-call | tf_op jit(solution)/shard_map/pallas_call | solution.py:392
  28.2 1.7 %copy.7 = f32[4,64,256]{2,1,0:T(8,128)} copy(f32[4,64,256]{2,1,0:T(8,128)} %shard_map.55) | data formatting | bytes 524288
